TPU v7x, 512 devices: a whole 4x4x16 slice. The times are simulated.
512 devices in a mesh: frames: 32 (over y, x, core), atoms: 16 (over z).
Axes of the slice: x: 4, y: 4, z: 16, core: 2. Of those that a mesh axis runs over, the one named last changes fastest.
Arguments:
- frames: float32 [2048, 3, 6144], P('frames', None, 'atoms'), may hold values from -45 to 45, as said below
- reference_structure: float32 [3, 6144], P(None, 'atoms'), may hold values from -15 to 15
Outputs:
- covariance: float32 [3, 6144, 3, 6144], P(None, 'frames', None, 'atoms')
- mean_structure: float32 [3, 6144], P(None, 'atoms')
Inputs may be any that keep to these rules, and one draw needn't show every extreme that they name: `frames`: every frame, once centered, has a cross-covariance with the centered reference_structure of positive determinant whose singular values lie within a factor of 20 of one another.
All inputs are finite; a program needn't handle non-finite values.
Results may differ from a plain program's by a relative error of at most 0.0003.
Values may be sent and summed in bfloat16 or wider, within the bound.
A program may use at most 64 MiB of HBM per device.

v0:
```python
import jax
import jax.numpy as jnp
from jax import lax
from jax.sharding import Mesh
from jax.sharding import PartitionSpec as P

ATOMS = 6144
ITERS = 2
POLAR = 8
FRAMES = ("frames_0", "frames_1", "frames_2")


def copy_for_each(array, axis):
    copies = jnp.broadcast_to(array, (lax.axis_size(axis), *array.shape))
    return lax.all_to_all(copies, axis, split_axis=0, concat_axis=0, tiled=True)


def over_copies(array, axis):
    everything = copy_for_each(array, axis)
    return jnp.sum(everything, axis=0)


def in_one(arrays, axis):
    vector, at, finished = (jnp.concatenate([a.reshape(-1) for a in arrays]), 0, [])
    total = over_copies(vector, axis)
    for a in arrays:
        finished.append(total[at : at + a.size].reshape(a.shape))
        at += a.size
    return tuple(finished)


def in_blocks(array, dim, devices):
    lengths = array.shape
    blocks = array.reshape(*lengths[:dim], devices, lengths[dim] // devices, *lengths[dim + 1 :])
    return jnp.moveaxis(blocks, dim, 0)


def laid_out(blocks, dim):
    blocks = jnp.moveaxis(blocks, 0, dim)
    lengths = blocks.shape
    return blocks.reshape(*lengths[:dim], lengths[dim] * lengths[dim + 1], *lengths[dim + 2 :])


def exchange_in_order(blocks, axes, turns):
    lengths = [lax.axis_size(a) for a in axes]
    blocks = blocks.reshape(*lengths, *blocks.shape[1:])
    for k in turns:
        blocks = lax.all_to_all(blocks, axes[k], split_axis=k, concat_axis=k, tiled=True)
    return blocks.reshape(-1, *blocks.shape[len(axes) :])


def core_and_chips(array, groups, turns, split_dim, concat_dim):
    devices = lax.axis_size(groups[0]) * lax.axis_size(groups[1])
    blocks = in_blocks(array, split_dim, devices)
    return laid_out(exchange_in_order(blocks, groups, turns), concat_dim)


def polar_factor(cross):
    factor = jnp.sqrt(3.0 / jnp.sum(cross * cross, axis=(0, 1)))
    matrix = cross * factor[None, None, :]
    for turn in range(POLAR):
        entries = [[matrix[i, j] for j in range(3)] for i in range(3)]
        cofactor = [
            [
                entries[(i + 1) % 3][(j + 1) % 3] * entries[(i + 2) % 3][(j + 2) % 3]
                - entries[(i + 1) % 3][(j + 2) % 3] * entries[(i + 2) % 3][(j + 1) % 3]
                for j in range(3)
            ]
            for i in range(3)
        ]
        determinant = (
            entries[0][0] * cofactor[0][0]
            + entries[0][1] * cofactor[0][1]
            + entries[0][2] * cofactor[0][2]
        )
        inverse = jnp.stack([jnp.stack(cofactor[i]) for i in range(3)]) / determinant[None, None, :]
        matrix = 0.5 * (matrix + inverse)
    return matrix


def contract_frames(left_rows, right_rows):
    return lax.dot_general(
        left_rows, right_rows, (((0,), (0,)), ((), ())), preferred_element_type=jnp.float32
    )


def body(frames, reference_structure):
    highest = lax.Precision.HIGHEST
    mean_now = reference_structure
    count_all = frames.shape[0] * lax.axis_size(FRAMES)
    for iteration in range(ITERS):
        sum_coords, sum_cross, sum_mean = in_one(
            (
                jnp.sum(frames, axis=2),
                jnp.einsum("fca,da->cdf", frames, mean_now, precision=highest),
                jnp.sum(mean_now, axis=1),
            ),
            "atoms",
        )
        centroid = sum_coords / ATOMS
        cross = sum_cross - centroid.T[:, None, :] * sum_mean[None, :, None]
        shifted = frames - centroid[:, :, None]
        rotation = polar_factor(cross)
        aligned = jnp.einsum("cdf,fca->fda", rotation, shifted, precision=highest)
        mean_now = over_copies(jnp.sum(aligned, axis=0), FRAMES) / count_all
    deviation = (aligned - mean_now[None]).astype(jnp.bfloat16)
    column_atoms = frames.shape[2]
    row_count = column_atoms * lax.axis_size("atoms") // lax.axis_size(FRAMES)
    own_rows = lax.all_gather(deviation, "atoms", axis=2, tiled=True)
    row_panel = core_and_chips(own_rows, (("frames_0", "frames_1"), "frames_2"), (1, 0), 2, 0)
    row_flat = row_panel.reshape(row_panel.shape[0], 3 * row_count)
    piece = lax.all_gather(deviation, FRAMES, axis=0, tiled=True)
    product = contract_frames(row_flat, piece.reshape(piece.shape[0], 3 * column_atoms))
    covariance = (product / count_all).reshape(3, row_count, 3, column_atoms)
    return (covariance, mean_now)


def solution(mesh):
    finer = Mesh(
        mesh.devices.reshape(4, 4, 2, mesh.shape["atoms"]),
        ("frames_0", "frames_1", "frames_2", "atoms"),
    )
    return jax.shard_map(
        body,
        mesh=finer,
        in_specs=(P(FRAMES, None, "atoms"), P(None, "atoms")),
        out_specs=(P(None, FRAMES, None, "atoms"), P(None, "atoms")),
        check_vma=False,
    )
```

profile of v0, /device:TPU:2, one launch (start us, length us, event | category | flops | bytes accessed | tf_op | source)
XLA Modules:
  0.0 281.3 jit_solution(8115866642797572257)
XLA Ops:
  7.2 0.8 reduce_sum.99
  8.1 1.1 reduce_sum.98
  9.1 1.4 convolution_bitcast_fusion.2
  10.6 0.1 reshape.5854
  10.7 0.1 copy.45
  10.8 0.1 reshape.5853
  11.1 27.7 %all_to_all.32 = f32[16,1,771]{2,1,0:T(1,128)S(1)} all-to-all(f32[16,1,771]{2,1,0:T(1,128)S(1)} %broadcast_in_dim.8), channel_id=1, replica_groups=mesh['frames_0'=4,'frames_1'=4,'frames_2'=2,'atoms'=16] {'atoms'}, dimensions={0} | all-to-all | bytes 98688 | tf_op jit(solution)/shard_map/all_to_all | solution.py:15
  39.0 0.1 div.197
  39.3 0.1 multiply_reduce_fusion.1
  39.9 0.1 fusion.9
  40.0 0.1 fusion.10
  40.2 0.1 fusion.11
  40.4 0.1 fusion.12
  40.5 0.1 fusion.13
  40.7 1.3 convolution_bitcast_fusion.1
  42.1 14.4 %all_to_all.33 = f32[32,3,384]{2,1,0:T(4,128)S(1)} all-to-all(f32[32,3,384]{2,1,0:T(4,128)S(1)} %broadcast_in_dim.9), channel_id=1, replica_groups=mesh['frames_0'=4,'frames_1'=4,'frames_2'=2,'atoms'=16] {'frames_0','fra..., dimensions={0} | all-to-all | bytes 294912 | tf_op jit(solution)/shard_map/all_to_all | solution.py:15
  56.6 0.1 multiply_reduce_fusion.2
  56.7 1.4 convolution_bitcast_fusion
  58.1 0.1 reshape.5856
  58.4 15.9 %all_to_all.34 = f32[16,1,771]{2,1,0:T(1,128)S(1)} all-to-all(f32[16,1,771]{2,1,0:T(1,128)S(1)} %broadcast_in_dim.10), channel_id=1, replica_groups=mesh['frames_0'=4,'frames_1'=4,'frames_2'=2,'atoms'=16] {'atoms'}, dimensions={0} | all-to-all | bytes 98688 | tf_op jit(solution)/shard_map/all_to_all | solution.py:15
  74.5 0.1 div.225
  74.8 0.1 multiply_reduce_fusion
  75.4 0.1 fusion.16
  75.5 0.1 fusion.17
  75.7 0.1 fusion.18
  75.9 0.1 fusion.19
  76.0 0.1 fusion.20
  76.2 0.1 fusion.21
  76.4 0.1 copy.53
  76.5 0.1 broadcast_subtract_fusion
  76.6 1.1 fusion.33
  77.7 11.5 %all_to_all.35 = f32[32,3,384]{2,1,0:T(4,128)S(1)} all-to-all(f32[32,3,384]{2,1,0:T(4,128)S(1)} %broadcast_in_dim.11), channel_id=1, replica_groups=mesh['frames_0'=4,'frames_1'=4,'frames_2'=2,'atoms'=16] {'frames_0','fra..., dimensions={0} | all-to-all | bytes 294912 | tf_op jit(solution)/shard_map/all_to_all | solution.py:15
  89.3 0.7 subtract_convert_fusion
  90.1 1.6 copy.60
  91.7 75.2 %all-gather.3.cloned.1.call-done = bf16[64,3,6144]{2,1,0:T(4,128)(2,1)} async-done(((bf16[64,3,384]{2,1,0:T(4,128)(2,1)}), bf16[64,3,6144]{2,1,0:T(4,128)(2,1)}) %all-gather.3.cloned.1.call-update) | async-done | bytes 2359312 | tf_op jit(solution)/shard_map/all_gather | solution.py:109
  166.9 3.6 %copy.56 = bf16[64,3,6144]{2,0,1:T(8,128)(2,1)S(1)} copy(bf16[64,3,6144]{2,1,0:T(4,128)(2,1)} %all-gather.3.cloned.1.call-done) | data formatting | bytes 4718592 | tf_op jit(solution)/shard_map/all_gather | solution.py:109
  170.5 4.6 %reshape.5858 = bf16[64,3,32,192]{3,2,0,1:T(8,128)(2,1)} reshape(bf16[64,3,6144]{2,0,1:T(8,128)(2,1)S(1)} %copy.56) | data formatting | bytes 4718592 | tf_op jit(solution)/shard_map/reshape | solution.py:34
  175.1 4.3 %reshape.5859 = bf16[16,2,64,3,192]{4,1,0,2,3:T(2,128)(2,1)S(1)} reshape(bf16[32,64,3,192]{3,0,1,2:T(8,128)(2,1)} %bitcast.395) | data formatting | bytes 4718592 | tf_op jit(solution)/shard_map/reshape | solution.py:46
  179.4 1.8 copy.57
  181.2 6.3 %all_to_all.36 = bf16[16,2,64,3,192]{4,2,3,0,1:T(8,128)(2,1)S(1)} all-to-all(bf16[16,2,64,3,192]{4,2,3,0,1:T(8,128)(2,1)S(1)} %copy.57), channel_id=1, replica_groups=mesh['frames_0'=4,'frames_1'=4,'frames_2'=2,'atoms'=16] {'frames_2'}, dimensions={1} | all-to-all | bytes 4718592 | tf_op jit(solution)/shard_map/all_to_all | solution.py:48
  187.4 0.4 copy.58
  187.8 53.9 %all_to_all.37 = bf16[16,2,64,3,192]{4,2,3,1,0:T(8,128)(2,1)S(1)} all-to-all(bf16[16,2,64,3,192]{4,2,3,1,0:T(8,128)(2,1)S(1)} %copy.58), channel_id=1, replica_groups=mesh['frames_0'=4,'frames_1'=4,'frames_2'=2,'atoms'=16] {'frames_0','fra..., dimensions={0} | all-to-all | bytes 4718592 | tf_op jit(solution)/shard_map/all_to_all | solution.py:48
  241.7 5.0 %copy.59 = bf16[16,2,64,3,192]{4,3,2,1,0:T(4,128)(2,1)} copy(bf16[16,2,64,3,192]{4,2,3,1,0:T(8,128)(2,1)S(1)} %all_to_all.37) | data formatting | bytes 4718592 | tf_op jit(solution)/shard_map/all_to_all | solution.py:48
  246.8 8.0 %reshape_reshape_reshape.3 = bf16[2048,576]{1,0:T(8,128)(2,1)S(1)} reshape(bf16[16,2,64,3,192]{4,3,2,1,0:T(4,128)(2,1)} %copy.59) | data formatting | bytes 4718592 | tf_op jit(solution)/shard_map/reshape;reshape;reshape | solution.py:111
  254.8 6.7 %copy.61 = bf16[2048,3,384]{0,2,1:T(8,128)(2,1)} copy(bf16[2048,3,384]{2,0,1:T(8,128)(2,1)} %all-gather.5.cloned.1.call-done) | data formatting | bytes 9437184 | tf_op jit(solution)/shard_map/all_gather | solution.py:112
  261.6 7.4 %convolution_multiply_fusion = f32[576,1152]{1,0:T(8,128)} fusion(bf16[2048,576]{1,0:T(8,128)(2,1)S(1)} %reshape_reshape_reshape.3, bf16[2048,1152]{0,1:T(8,128)(2,1)} %bitcast.396), kind=kOutput, calls=%fused_computation | convolution fusion | flops 2718572544 | bytes 9732096 | tf_op jit(solution)/shard_map/dot_general | solution.py:82
  269.0 3.7 %reshape.5861 = f32[3,192,3,384]{3,2,1,0:T(4,128)S(1)} reshape(f32[576,1152]{1,0:T(8,128)} %convolution_multiply_fusion) | data formatting | bytes 5308416 | tf_op jit(solution)/shard_map/reshape | solution.py:114
  272.7 1.7 copy.62
  (119 shorter events, 2.6 us)
Async XLA Ops:
  7.2 69.3 %copy-start = (f32[64,3,384]{2,0,1:T(8,128)S(1)}, f32[64,3,384]{2,0,1:T(8,128)}, u32[]{:S(2)}) copy-start(f32[64,3,384]{2,0,1:T(8,128)} %param.2) | copy-start | bytes 884740
  7.2 159.8 %all-gather.3.cloned.1.call-start = ((), (), s32[]{:S(2)}) async-start(), calls=%async_computation.6 | async-start | bytes 3342336 | tf_op jit(solution)/shard_map/all_gather | solution.py:109
  89.3 81.3 %copy-start.1 = (f32[3,384]{1,0:T(4,128)}, f32[3,384]{1,0:T(4,128)S(1)}, u32[]{:S(2)}) copy-start(f32[3,384]{1,0:T(4,128)S(1)} %broadcast_multiply_fusion) | copy-start | bytes 13828
  90.1 164.8 %all-gather.5.cloned.1.call-start = ((), (), s32[]{:S(2)}) async-start(), calls=%async_computation.7 | async-start | bytes 4866048 | tf_op jit(solution)/shard_map/all_gather | solution.py:112
Sparse Core Ops, SparseCore 0:
  90.2 76.7 all-gather.2
  170.1 73.4 all-gather.4
where the time goes:
time: 282 us; the launch traced here: 281 us
  blocking collectives  130 us (46%)
  waiting for transfers between devices  75.2 us (27%)
  local copies, waits for them, and re-layouts  43.1 us (15%)
  between operations  14.7 us (5%)
  matrix products  12.7 us (5%)
  other arithmetic  5.79 us (2%)
    all_gather x1, waiting for transfers between devices, body(): own_rows = lax.all_gather(deviation, 'atoms', axis=2, tiled=True)  75.2 us
    all_to_all x4, blocking collectives, copy_for_each(): return lax.all_to_all(copies, axis, split_axis=0, concat_axis=0, tiled=True)  69.5 us
    all_to_all x2, blocking collectives, exchange_in_order(): lax.all_to_all(blocks, axes[k], split_axis=k, concat_axis=k, tiled=True)  60.2 us
    another operation x1, local copies, waits for them, and re-layouts, body(): row_flat = row_panel.reshape(row_panel.shape[0], 3 * row_count)  8.03 us
    dot_general x1, matrix products, contract_frames(): lax.dot_general(left_rows, right_rows, (((0,), (0,)), ((), ())), preferre...  7.42 us
    all_gather x1, local copies, waits for them, and re-layouts, body(): piece = lax.all_gather(deviation, FRAMES, axis=0, tiled=True)  6.75 us
    reshape x2, local copies, waits for them, and re-layouts, exchange_in_order(): blocks = blocks.reshape(*lengths, *blocks.shape[1:])  6.04 us
  transfers between devices with their start and end apart: 2, of which 1 were waited for; matrix products, arithmetic and copies ran while one was open for 10% of the time, Pallas kernels for 0%

commit v1 on v0

--- a/solution.py
+++ b/solution.py
@@ -106,7 +106,23 @@
     deviation = (aligned - mean_now[None]).astype(jnp.bfloat16)
     column_atoms = frames.shape[2]
     row_count = column_atoms * lax.axis_size("atoms") // lax.axis_size(FRAMES)
-    own_rows = lax.all_gather(deviation, "atoms", axis=2, tiled=True)
+    ways, here, step = (lax.axis_size("atoms"), lax.axis_index("atoms"), deviation.shape[2])
+    dims = [n * ways if d == 2 else n for d, n in enumerate(deviation.shape)]
+    full = lax.dynamic_update_slice_in_dim(
+        jnp.zeros(dims, deviation.dtype), deviation, here * step, axis=2
+    )
+    going_up = going_down = deviation
+    for far in range(1, ways // 2 + 1):
+        going_up = lax.ppermute(going_up, "atoms", [(d, (d + 1) % ways) for d in range(ways)])
+        full = lax.dynamic_update_slice_in_dim(full, going_up, (here - far) % ways * step, axis=2)
+        if 2 * far < ways:
+            going_down = lax.ppermute(
+                going_down, "atoms", [(d, (d - 1) % ways) for d in range(ways)]
+            )
+            full = lax.dynamic_update_slice_in_dim(
+                full, going_down, (here + far) % ways * step, axis=2
+            )
+    own_rows = full
     row_panel = core_and_chips(own_rows, (("frames_0", "frames_1"), "frames_2"), (1, 0), 2, 0)
     row_flat = row_panel.reshape(row_panel.shape[0], 3 * row_count)
     piece = lax.all_gather(deviation, FRAMES, axis=0, tiled=True)

time: 282 us -> 270 us (0.957)
  the two profiles are of different devices: /device:TPU:2 before, /device:TPU:1 now
where the time goes in v1:
time: 270 us; the launch traced here: 269 us
  blocking collectives  116 us (43%)
  starting transfers between devices  54.4 us (20%)
  local copies, waits for them, and re-layouts  40.1 us (15%)
  waiting for transfers between devices  26.6 us (10%)
  between operations  15.3 us (6%)
  matrix products  11.8 us (4%)
  other arithmetic  5.13 us (2%)
    all_to_all x3, blocking collectives, copy_for_each(): return lax.all_to_all(copies, axis, split_axis=0, concat_axis=0, tiled=True)  58.5 us
    all_to_all x2, blocking collectives, exchange_in_order(): lax.all_to_all(blocks, axes[k], split_axis=k, concat_axis=k, tiled=True)  57.2 us
    ppermute x7, starting transfers between devices, body(): lax.ppermute(going_down, 'atoms', [(d, (d - 1) % ways) for d in range(way...  33.3 us
    ppermute x8, starting transfers between devices, body(): lax.ppermute(going_up, 'atoms', [(d, (d + 1) % ways) for d in range(ways)])  15.7 us
    ppermute x8, waiting for transfers between devices, body(): lax.ppermute(going_up, 'atoms', [(d, (d + 1) % ways) for d in range(ways)])  12.1 us
    all_to_all x1, waiting for transfers between devices, copy_for_each(): return lax.all_to_all(copies, axis, split_axis=0, concat_axis=0, tiled=True)  8.32 us
    another operation x1, local copies, waits for them, and re-layouts, body(): row_flat = row_panel.reshape(row_panel.shape[0], 3 * row_count)  8.03 us
    dot_general x1, matrix products, contract_frames(): lax.dot_general(left_rows, right_rows, (((0,), (0,)), ((), ())), preferre...  7.42 us
  transfers between devices with their start and end apart: 17, of which 9 were waited for; matrix products, arithmetic and copies ran while one was open for 9% of the time, Pallas kernels for 0%

profile of v1, /device:TPU:1, one launch (start us, length us, event | category | flops | bytes accessed | tf_op | source)
XLA Modules:
  0.0 269.0 jit_solution(2425342773651873030)
XLA Ops:
  7.2 0.9 reduce_sum.99
  8.0 1.1 reduce_sum.98
  9.1 1.4 convolution_bitcast_fusion.2
  11.0 27.2 %all_to_all.32 = f32[16,1,771]{2,1,0:T(1,128)S(1)} all-to-all(f32[16,1,771]{2,1,0:T(1,128)S(1)} %broadcast_in_dim.11), channel_id=1, replica_groups=mesh['frames_0'=4,'frames_1'=4,'frames_2'=2,'atoms'=16] {'atoms'}, dimensions={0} | all-to-all | bytes 98688 | tf_op jit(solution)/shard_map/all_to_all | solution.py:15
  40.2 1.3 convolution_bitcast_fusion.1
  41.5 17.2 %all_to_all.33 = f32[32,3,384]{2,1,0:T(4,128)S(1)} all-to-all(f32[32,3,384]{2,1,0:T(4,128)S(1)} %broadcast_in_dim.12), channel_id=1, replica_groups=mesh['frames_0'=4,'frames_1'=4,'frames_2'=2,'atoms'=16] {'frames_0','fra..., dimensions={0} | all-to-all | bytes 294912 | tf_op jit(solution)/shard_map/all_to_all | solution.py:15
  58.9 0.5 convolution_bitcast_fusion
  59.6 14.2 %all_to_all.34 = f32[16,1,771]{2,1,0:T(1,128)S(1)} all-to-all(f32[16,1,771]{2,1,0:T(1,128)S(1)} %broadcast_in_dim.13), channel_id=1, replica_groups=mesh['frames_0'=4,'frames_1'=4,'frames_2'=2,'atoms'=16] {'atoms'}, dimensions={0} | all-to-all | bytes 98688 | tf_op jit(solution)/shard_map/all_to_all | solution.py:15
  76.1 1.1 fusion.33
  77.2 0.7 broadcast_in_dim.14
  77.9 5.4 %all-to-all-start.3 = ((f32[32,3,384]{2,1,0:T(4,128)}), f32[32,3,384]{2,1,0:T(4,128)S(1)}, u32[]{:S(2)}, u32[]{:S(2)}) async-start(f32[32,3,384]{2,1,0:T(4,128)} %broadcast_in_dim.14), calls=%async_computation.3 | async-start | bytes 393216 | tf_op jit(solution)/shard_map/all_to_all | solution.py:15
  83.4 8.3 %all-to-all-done.3 = f32[32,3,384]{2,1,0:T(4,128)S(1)} async-done(((f32[32,3,384]{2,1,0:T(4,128)}), f32[32,3,384]{2,1,0:T(4,128)S(1)}, u32[]{:S(2)}, u32[]{:S(2)}) %all-to-all-start.3) | async-done | bytes 147488 | tf_op jit(solution)/shard_map/all_to_all | solution.py:15
  92.1 0.7 constant_dynamic-update-slice_fusion
  92.8 3.0 %collective-permute-start.1 = (bf16[64,3,384]{2,1,0:T(4,128)(2,1)S(1)}, bf16[64,3,384]{2,1,0:T(4,128)(2,1)S(1)}, u32[]{:S(2)}, u32[]{:S(2)}) collective-permute-start(bf16[64,3,384]{2,1,0:T(4,128)(2,1)S(1)} %subtract_convert_fusion), channel_id=1, source_target_pairs={{0,15},{1,0},{2,1},{3,2},{4,3},{5,4},{6,5},{7,6},{8,7},{9,8},{10,9... | collective-permute-start | bytes 442376 | tf_op jit(solution)/shard_map/ppermute | solution.py:119
  95.8 2.3 collective-permute-start
  98.4 2.7 collective-permute-done.1
  101.1 4.2 %collective-permute-start.3 = (bf16[64,3,384]{2,1,0:T(4,128)(2,1)S(1)}, bf16[64,3,384]{2,1,0:T(4,128)(2,1)S(1)}, u32[]{:S(2)}, u32[]{:S(2)}) collective-permute-start(bf16[64,3,384]{2,1,0:T(4,128)(2,1)S(1)} %collective-permute-done.1), channel_id=1, source_target_pairs={{0,15},{1,0},{2,1},{3,2},{4,3},{5,4},{6,5},{7,6},{8,7},{9,8},{10,9... | collective-permute-start | bytes 442376 | tf_op jit(solution)/shard_map/ppermute | solution.py:119
  105.3 1.9 collective-permute-start.2
  107.3 1.2 collective-permute-done.3
  108.5 5.3 %collective-permute-start.5 = (bf16[64,3,384]{2,1,0:T(4,128)(2,1)S(1)}, bf16[64,3,384]{2,1,0:T(4,128)(2,1)S(1)}, u32[]{:S(2)}, u32[]{:S(2)}) collective-permute-start(bf16[64,3,384]{2,1,0:T(4,128)(2,1)S(1)} %collective-permute-done.3), channel_id=1, source_target_pairs={{0,15},{1,0},{2,1},{3,2},{4,3},{5,4},{6,5},{7,6},{8,7},{9,8},{10,9... | collective-permute-start | bytes 442376 | tf_op jit(solution)/shard_map/ppermute | solution.py:119
  113.8 1.9 collective-permute-start.4
  115.9 0.6 collective-permute-done.5
  116.4 5.0 %collective-permute-start.7 = (bf16[64,3,384]{2,1,0:T(4,128)(2,1)S(1)}, bf16[64,3,384]{2,1,0:T(4,128)(2,1)S(1)}, u32[]{:S(2)}, u32[]{:S(2)}) collective-permute-start(bf16[64,3,384]{2,1,0:T(4,128)(2,1)S(1)} %collective-permute-done.5), channel_id=1, source_target_pairs={{0,15},{1,0},{2,1},{3,2},{4,3},{5,4},{6,5},{7,6},{8,7},{9,8},{10,9... | collective-permute-start | bytes 442376 | tf_op jit(solution)/shard_map/ppermute | solution.py:119
  121.5 1.9 collective-permute-start.6
  123.5 0.6 collective-permute-done.7
  124.0 5.0 %collective-permute-start.9 = (bf16[64,3,384]{2,1,0:T(4,128)(2,1)S(1)}, bf16[64,3,384]{2,1,0:T(4,128)(2,1)S(1)}, u32[]{:S(2)}, u32[]{:S(2)}) collective-permute-start(bf16[64,3,384]{2,1,0:T(4,128)(2,1)S(1)} %collective-permute-done.7), channel_id=1, source_target_pairs={{0,15},{1,0},{2,1},{3,2},{4,3},{5,4},{6,5},{7,6},{8,7},{9,8},{10,9... | collective-permute-start | bytes 442376 | tf_op jit(solution)/shard_map/ppermute | solution.py:119
  129.1 1.9 collective-permute-start.8
  131.1 0.6 collective-permute-done.9
  131.7 5.4 %collective-permute-start.11 = (bf16[64,3,384]{2,1,0:T(4,128)(2,1)S(1)}, bf16[64,3,384]{2,1,0:T(4,128)(2,1)S(1)}, u32[]{:S(2)}, u32[]{:S(2)}) collective-permute-start(bf16[64,3,384]{2,1,0:T(4,128)(2,1)S(1)} %collective-permute-done.9), channel_id=1, source_target_pairs={{0,15},{1,0},{2,1},{3,2},{4,3},{5,4},{6,5},{7,6},{8,7},{9,8},{10,9... | collective-permute-start | bytes 442376 | tf_op jit(solution)/shard_map/ppermute | solution.py:119
  137.1 1.9 collective-permute-start.10
  139.1 0.6 collective-permute-done.11
  139.7 5.4 %collective-permute-start.13 = (bf16[64,3,384]{2,1,0:T(4,128)(2,1)S(1)}, bf16[64,3,384]{2,1,0:T(4,128)(2,1)S(1)}, u32[]{:S(2)}, u32[]{:S(2)}) collective-permute-start(bf16[64,3,384]{2,1,0:T(4,128)(2,1)S(1)} %collective-permute-done.11), channel_id=1, source_target_pairs={{0,15},{1,0},{2,1},{3,2},{4,3},{5,4},{6,5},{7,6},{8,7},{9,8},{10,9... | collective-permute-start | bytes 442376 | tf_op jit(solution)/shard_map/ppermute | solution.py:119
  145.1 1.9 collective-permute-start.12
  147.1 5.6 %collective-permute-done.12 = bf16[64,3,384]{2,1,0:T(4,128)(2,1)S(1)} collective-permute-done((bf16[64,3,384]{2,1,0:T(4,128)(2,1)S(1)}, bf16[64,3,384]{2,1,0:T(4,128)(2,1)S(1)}, u32[]{:S(2)}, u32[]{:S(2)}) %collective-permute-start.12) | collective-permute-done | bytes 147488 | tf_op jit(solution)/shard_map/ppermute | solution.py:116
  152.7 1.9 collective-permute-start.14
  154.7 6.4 %collective-permute-done.14 = bf16[64,3,384]{2,1,0:T(4,128)(2,1)S(1)} collective-permute-done((bf16[64,3,384]{2,1,0:T(4,128)(2,1)S(1)}, bf16[64,3,384]{2,1,0:T(4,128)(2,1)S(1)}, u32[]{:S(2)}, u32[]{:S(2)}) %collective-permute-start.14) | collective-permute-done | bytes 147488 | tf_op jit(solution)/shard_map/ppermute | solution.py:116
  161.2 4.5 %reshape.5858 = bf16[64,3,32,192]{3,2,0,1:T(8,128)(2,1)} reshape(bf16[64,3,6144]{2,0,1:T(8,128)(2,1)S(1)} %copy_dynamic-update-slice_fusion) | data formatting | bytes 4718592 | tf_op jit(solution)/shard_map/reshape | solution.py:34
  165.8 4.3 %reshape.5859 = bf16[16,2,64,3,192]{4,1,0,2,3:T(2,128)(2,1)S(1)} reshape(bf16[32,64,3,192]{3,0,1,2:T(8,128)(2,1)} %bitcast.395) | data formatting | bytes 4718592 | tf_op jit(solution)/shard_map/reshape | solution.py:46
  170.1 1.8 copy.117
  171.8 14.0 %all_to_all.35 = bf16[16,2,64,3,192]{4,2,3,0,1:T(8,128)(2,1)S(1)} all-to-all(bf16[16,2,64,3,192]{4,2,3,0,1:T(8,128)(2,1)S(1)} %copy.117), channel_id=1, replica_groups=mesh['frames_0'=4,'frames_1'=4,'frames_2'=2,'atoms'=16] {'frames_2'}, dimensions={1} | all-to-all | bytes 4718592 | tf_op jit(solution)/shard_map/all_to_all | solution.py:48
  185.9 0.4 copy.118
  186.3 43.1 %all_to_all.36 = bf16[16,2,64,3,192]{4,2,3,1,0:T(8,128)(2,1)S(1)} all-to-all(bf16[16,2,64,3,192]{4,2,3,1,0:T(8,128)(2,1)S(1)} %copy.118), channel_id=1, replica_groups=mesh['frames_0'=4,'frames_1'=4,'frames_2'=2,'atoms'=16] {'frames_0','fra..., dimensions={0} | all-to-all | bytes 4718592 | tf_op jit(solution)/shard_map/all_to_all | solution.py:48
  229.4 5.0 %copy.119 = bf16[16,2,64,3,192]{4,3,2,1,0:T(4,128)(2,1)} copy(bf16[16,2,64,3,192]{4,2,3,1,0:T(8,128)(2,1)S(1)} %all_to_all.36) | data formatting | bytes 4718592 | tf_op jit(solution)/shard_map/all_to_all | solution.py:48
  234.4 8.0 %reshape_reshape_reshape.3 = bf16[2048,576]{1,0:T(8,128)(2,1)S(1)} reshape(bf16[16,2,64,3,192]{4,3,2,1,0:T(4,128)(2,1)} %copy.119) | data formatting | bytes 4718592 | tf_op jit(solution)/shard_map/reshape;reshape;reshape | solution.py:127
  242.5 6.7 %copy.121 = bf16[2048,3,384]{0,2,1:T(8,128)(2,1)} copy(bf16[2048,3,384]{2,0,1:T(8,128)(2,1)} %all-gather.2.cloned.1.call-done) | data formatting | bytes 9437184 | tf_op jit(solution)/shard_map/all_gather | solution.py:128
  249.2 7.4 %convolution_multiply_fusion = f32[576,1152]{1,0:T(8,128)} fusion(bf16[2048,576]{1,0:T(8,128)(2,1)S(1)} %reshape_reshape_reshape.3, bf16[2048,1152]{0,1:T(8,128)(2,1)} %bitcast.396), kind=kOutput, calls=%fused_computation | convolution fusion | flops 2718572544 | bytes 9732096 | tf_op jit(solution)/shard_map/dot_general | solution.py:82
  256.7 3.7 %reshape.5861 = f32[3,192,3,384]{3,2,1,0:T(4,128)S(1)} reshape(f32[576,1152]{1,0:T(8,128)} %convolution_multiply_fusion) | data formatting | bytes 5308416 | tf_op jit(solution)/shard_map/reshape | solution.py:130
  260.4 1.7 copy.122
  (162 shorter events, 5.8 us)
Async XLA Ops:
  7.2 51.7 %copy-start = (f32[64,3,384]{2,0,1:T(8,128)S(1)}, f32[64,3,384]{2,0,1:T(8,128)}, u32[]{:S(2)}) copy-start(f32[64,3,384]{2,0,1:T(8,128)} %param.2) | copy-start | bytes 884740
  77.9 13.8 %all-to-all-start.3 = ((f32[32,3,384]{2,1,0:T(4,128)}), f32[32,3,384]{2,1,0:T(4,128)S(1)}, u32[]{:S(2)}, u32[]{:S(2)}) async-start(f32[32,3,384]{2,1,0:T(4,128)} %broadcast_in_dim.14), calls=%async_computation.3 | async-start | bytes 393216 | tf_op jit(solution)/shard_map/all_to_all | solution.py:15
  83.3 159.2 %all-gather.2.cloned.1.call-start = ((), (), s32[]{:S(2)}) async-start(), calls=%async_computation.6 | async-start | bytes 4866048 | tf_op jit(solution)/shard_map/all_gather | solution.py:128
  91.8 15.5 %copy-start.1 = (f32[3,384]{1,0:T(4,128)}, f32[3,384]{1,0:T(4,128)S(1)}, u32[]{:S(2)}) copy-start(f32[3,384]{1,0:T(4,128)S(1)} %broadcast_multiply_fusion) | copy-start | bytes 13828
  92.8 8.2 %collective-permute-start.1 = (bf16[64,3,384]{2,1,0:T(4,128)(2,1)S(1)}, bf16[64,3,384]{2,1,0:T(4,128)(2,1)S(1)}, u32[]{:S(2)}, u32[]{:S(2)}) collective-permute-start(bf16[64,3,384]{2,1,0:T(4,128)(2,1)S(1)} %subtract_convert_fusion), channel_id=1, source_target_pairs={{0,15},{1,0},{2,1},{3,2},{4,3},{5,4},{6,5},{7,6},{8,7},{9,8},{10,9... | collective-permute-start | bytes 442376 | tf_op jit(solution)/shard_map/ppermute | solution.py:119
  95.8 9.4 %collective-permute-start = (bf16[64,3,384]{2,1,0:T(4,128)(2,1)S(1)}, bf16[64,3,384]{2,1,0:T(4,128)(2,1)S(1)}, u32[]{:S(2)}, u32[]{:S(2)}) collective-permute-start(bf16[64,3,384]{2,1,0:T(4,128)(2,1)S(1)} %subtract_convert_fusion), channel_id=1, source_target_pairs={{0,1},{1,2},{2,3},{3,4},{4,5},{5,6},{6,7},{7,8},{8,9},{9,10},{10,1... | collective-permute-start | bytes 442376 | tf_op jit(solution)/shard_map/ppermute | solution.py:116
  101.1 7.4 %collective-permute-start.3 = (bf16[64,3,384]{2,1,0:T(4,128)(2,1)S(1)}, bf16[64,3,384]{2,1,0:T(4,128)(2,1)S(1)}, u32[]{:S(2)}, u32[]{:S(2)}) collective-permute-start(bf16[64,3,384]{2,1,0:T(4,128)(2,1)S(1)} %collective-permute-done.1), channel_id=1, source_target_pairs={{0,15},{1,0},{2,1},{3,2},{4,3},{5,4},{6,5},{7,6},{8,7},{9,8},{10,9... | collective-permute-start | bytes 442376 | tf_op jit(solution)/shard_map/ppermute | solution.py:119
  105.3 8.6 %collective-permute-start.2 = (bf16[64,3,384]{2,1,0:T(4,128)(2,1)S(1)}, bf16[64,3,384]{2,1,0:T(4,128)(2,1)S(1)}, u32[]{:S(2)}, u32[]{:S(2)}) collective-permute-start(bf16[64,3,384]{2,1,0:T(4,128)(2,1)S(1)} %collective-permute-done), channel_id=1, source_target_pairs={{0,1},{1,2},{2,3},{3,4},{4,5},{5,6},{6,7},{7,8},{8,9},{9,10},{10,1... | collective-permute-start | bytes 442376 | tf_op jit(solution)/shard_map/ppermute | solution.py:116
  108.5 7.9 %collective-permute-start.5 = (bf16[64,3,384]{2,1,0:T(4,128)(2,1)S(1)}, bf16[64,3,384]{2,1,0:T(4,128)(2,1)S(1)}, u32[]{:S(2)}, u32[]{:S(2)}) collective-permute-start(bf16[64,3,384]{2,1,0:T(4,128)(2,1)S(1)} %collective-permute-done.3), channel_id=1, source_target_pairs={{0,15},{1,0},{2,1},{3,2},{4,3},{5,4},{6,5},{7,6},{8,7},{9,8},{10,9... | collective-permute-start | bytes 442376 | tf_op jit(solution)/shard_map/ppermute | solution.py:119
  113.8 7.6 %collective-permute-start.4 = (bf16[64,3,384]{2,1,0:T(4,128)(2,1)S(1)}, bf16[64,3,384]{2,1,0:T(4,128)(2,1)S(1)}, u32[]{:S(2)}, u32[]{:S(2)}) collective-permute-start(bf16[64,3,384]{2,1,0:T(4,128)(2,1)S(1)} %collective-permute-done.2), channel_id=1, source_target_pairs={{0,1},{1,2},{2,3},{3,4},{4,5},{5,6},{6,7},{7,8},{8,9},{9,10},{10,1... | collective-permute-start | bytes 442376 | tf_op jit(solution)/shard_map/ppermute | solution.py:116
  116.4 7.6 %collective-permute-start.7 = (bf16[64,3,384]{2,1,0:T(4,128)(2,1)S(1)}, bf16[64,3,384]{2,1,0:T(4,128)(2,1)S(1)}, u32[]{:S(2)}, u32[]{:S(2)}) collective-permute-start(bf16[64,3,384]{2,1,0:T(4,128)(2,1)S(1)} %collective-permute-done.5), channel_id=1, source_target_pairs={{0,15},{1,0},{2,1},{3,2},{4,3},{5,4},{6,5},{7,6},{8,7},{9,8},{10,9... | collective-permute-start | bytes 442376 | tf_op jit(solution)/shard_map/ppermute | solution.py:119
  121.5 7.6 %collective-permute-start.6 = (bf16[64,3,384]{2,1,0:T(4,128)(2,1)S(1)}, bf16[64,3,384]{2,1,0:T(4,128)(2,1)S(1)}, u32[]{:S(2)}, u32[]{:S(2)}) collective-permute-start(bf16[64,3,384]{2,1,0:T(4,128)(2,1)S(1)} %collective-permute-done.4), channel_id=1, source_target_pairs={{0,1},{1,2},{2,3},{3,4},{4,5},{5,6},{6,7},{7,8},{8,9},{9,10},{10,1... | collective-permute-start | bytes 442376 | tf_op jit(solution)/shard_map/ppermute | solution.py:116
  124.0 7.6 %collective-permute-start.9 = (bf16[64,3,384]{2,1,0:T(4,128)(2,1)S(1)}, bf16[64,3,384]{2,1,0:T(4,128)(2,1)S(1)}, u32[]{:S(2)}, u32[]{:S(2)}) collective-permute-start(bf16[64,3,384]{2,1,0:T(4,128)(2,1)S(1)} %collective-permute-done.7), channel_id=1, source_target_pairs={{0,15},{1,0},{2,1},{3,2},{4,3},{5,4},{6,5},{7,6},{8,7},{9,8},{10,9... | collective-permute-start | bytes 442376 | tf_op jit(solution)/shard_map/ppermute | solution.py:119
  129.1 8.0 %collective-permute-start.8 = (bf16[64,3,384]{2,1,0:T(4,128)(2,1)S(1)}, bf16[64,3,384]{2,1,0:T(4,128)(2,1)S(1)}, u32[]{:S(2)}, u32[]{:S(2)}) collective-permute-start(bf16[64,3,384]{2,1,0:T(4,128)(2,1)S(1)} %collective-permute-done.6), channel_id=1, source_target_pairs={{0,1},{1,2},{2,3},{3,4},{4,5},{5,6},{6,7},{7,8},{8,9},{9,10},{10,1... | collective-permute-start | bytes 442376 | tf_op jit(solution)/shard_map/ppermute | solution.py:116
  131.7 8.0 %collective-permute-start.11 = (bf16[64,3,384]{2,1,0:T(4,128)(2,1)S(1)}, bf16[64,3,384]{2,1,0:T(4,128)(2,1)S(1)}, u32[]{:S(2)}, u32[]{:S(2)}) collective-permute-start(bf16[64,3,384]{2,1,0:T(4,128)(2,1)S(1)} %collective-permute-done.9), channel_id=1, source_target_pairs={{0,15},{1,0},{2,1},{3,2},{4,3},{5,4},{6,5},{7,6},{8,7},{9,8},{10,9... | collective-permute-start | bytes 442376 | tf_op jit(solution)/shard_map/ppermute | solution.py:119
  137.1 8.0 %collective-permute-start.10 = (bf16[64,3,384]{2,1,0:T(4,128)(2,1)S(1)}, bf16[64,3,384]{2,1,0:T(4,128)(2,1)S(1)}, u32[]{:S(2)}, u32[]{:S(2)}) collective-permute-start(bf16[64,3,384]{2,1,0:T(4,128)(2,1)S(1)} %collective-permute-done.8), channel_id=1, source_target_pairs={{0,1},{1,2},{2,3},{3,4},{4,5},{5,6},{6,7},{7,8},{8,9},{9,10},{10,1... | collective-permute-start | bytes 442376 | tf_op jit(solution)/shard_map/ppermute | solution.py:116
  139.7 15.0 %collective-permute-start.13 = (bf16[64,3,384]{2,1,0:T(4,128)(2,1)S(1)}, bf16[64,3,384]{2,1,0:T(4,128)(2,1)S(1)}, u32[]{:S(2)}, u32[]{:S(2)}) collective-permute-start(bf16[64,3,384]{2,1,0:T(4,128)(2,1)S(1)} %collective-permute-done.11), channel_id=1, source_target_pairs={{0,15},{1,0},{2,1},{3,2},{4,3},{5,4},{6,5},{7,6},{8,7},{9,8},{10,9... | collective-permute-start | bytes 442376 | tf_op jit(solution)/shard_map/ppermute | solution.py:119
  145.1 7.6 %collective-permute-start.12 = (bf16[64,3,384]{2,1,0:T(4,128)(2,1)S(1)}, bf16[64,3,384]{2,1,0:T(4,128)(2,1)S(1)}, u32[]{:S(2)}, u32[]{:S(2)}) collective-permute-start(bf16[64,3,384]{2,1,0:T(4,128)(2,1)S(1)} %collective-permute-done.10), channel_id=1, source_target_pairs={{0,1},{1,2},{2,3},{3,4},{4,5},{5,6},{6,7},{7,8},{8,9},{9,10},{10,1... | collective-permute-start | bytes 442376 | tf_op jit(solution)/shard_map/ppermute | solution.py:116
  152.7 8.5 %collective-permute-start.14 = (bf16[64,3,384]{2,1,0:T(4,128)(2,1)S(1)}, bf16[64,3,384]{2,1,0:T(4,128)(2,1)S(1)}, u32[]{:S(2)}, u32[]{:S(2)}) collective-permute-start(bf16[64,3,384]{2,1,0:T(4,128)(2,1)S(1)} %collective-permute-done.12), channel_id=1, source_target_pairs={{0,1},{1,2},{2,3},{3,4},{4,5},{5,6},{6,7},{7,8},{8,9},{9,10},{10,1... | collective-permute-start | bytes 442376 | tf_op jit(solution)/shard_map/ppermute | solution.py:116
Sparse Core Ops, SparseCore 0:
  93.0 50.6 all-gather.1
